TPU v7x, 256 devices: a whole 4x4x8 slice. The times are simulated.
256 devices in a mesh: ctx: 32 (over y, z_lo, x), head: 8 (over z_hi, core).
Axes of the slice: x: 4, y: 4, z: 8 (z_hi: 4, z_lo: 2; z = z_hi * 2 + z_lo), core: 2. Of those that a mesh axis runs over, the one named last changes fastest.
Arguments:
- q_nope: bfloat16 [4096, 8192], P('ctx', 'head'), may hold values from -210 to 210
- q_rope: bfloat16 [4096, 4096], P('ctx', 'head'), may hold values from -6 to 6
- key_latent: bfloat16 [4096, 576], P(('ctx', 'head')), may hold values from -6 to 6
- doc_ids: int32 [4096], P(('ctx', 'head')), may hold values from 0 to 3, as said below
- doc_offsets: int32 [4], replicated, may hold values from 0 to 98303
- owners: int32 [4096, 1], P(('ctx', 'head')), may hold values from 0 to 31; in each aligned block of 128 rows (0 to 127, 128 to 255, ...) at most 8 rows name the same one
- w_key: bfloat16 [64, 128, 512], P('head'), may hold values from -0.5 to 0.5
- w_value: bfloat16 [64, 512, 128], P('head'), may hold values from -0.25 to 0.25
Outputs:
- attended: bfloat16 [4096, 8192], P('ctx', 'head')
- cache: bfloat16 [8192, 576], P(('ctx', 'head'))
Inputs may be any that keep to these rules, and one draw needn't show every extreme that they name: `doc_ids`: never falls; request 0 has exactly 2056 tokens, every other request 1 or more. `owners`: in each aligned block of 128 rows no owner is named by more than 8 rows; in some block some owner is named by exactly 8.
All inputs are finite; a program needn't handle non-finite values.
Results may differ from a plain program's by a relative error of at most 0.011.
Values may be sent and summed in bfloat16 or wider, within the bound.
A program may use at most 64 MiB of HBM per device.

v0:
```python
import jax
import jax.numpy as jnp
from jax import lax
from jax.sharding import PartitionSpec as P

NOPE = 128
ROPE = 64
LATENT = 512
VDIM = 128


def carried_in(part, axis, combine, identity):
    place = lax.axis_index(axis)
    gathered = lax.all_gather(part, axis)
    state = jnp.zeros_like(part) + jnp.asarray(identity, part.dtype)

    def one(lap, state):
        return combine(state, lax.dynamic_index_in_dim(gathered, lap, 0, False))

    return lax.fori_loop(0, place, one, state)


def rotate(values, positions):
    half = values.shape[-1] // 2
    steps = jnp.arange(half, dtype=jnp.float32)
    inverse = 10000.0 ** (-2.0 * steps / values.shape[-1])
    angle = positions.astype(jnp.float32)[..., None] * inverse
    first = values[..., :half]
    second = values[..., half:]
    cosine = jnp.cos(angle)
    sine = jnp.sin(angle)
    return jnp.concatenate([first * cosine - second * sine, first * sine + second * cosine], -1)


def dispatch(targets, values, owners_count, first_slot, slots_count):
    hits = (targets[:, None] == jnp.arange(owners_count, dtype=jnp.int32)[None, :]).astype(
        jnp.int32
    )
    slots = jnp.cumsum(hits, 0) - hits - first_slot
    place = (hits[:, :, None] == 1) & (
        slots[:, :, None] == jnp.arange(slots_count, dtype=jnp.int32)[None, None, :]
    )
    return jnp.einsum(
        "rnc,rd->ncd", place.astype(jnp.bfloat16), values, preferred_element_type=jnp.float32
    ).astype(jnp.bfloat16)


def add_counts(earlier_part, later_part):
    return earlier_part + later_part


def local(q_nope, q_rope, key_latent, doc_ids, doc_offsets, owners, w_key, w_value):
    reqs = doc_offsets.shape[0]
    n_ctx = lax.axis_size("ctx")
    n_head = lax.axis_size("head")
    hits = (doc_ids[:, None] == jnp.arange(reqs, dtype=jnp.int32)[None, :]).astype(jnp.int32)
    counts = jnp.sum(hits, 0)
    before = carried_in(counts, ("ctx", "head"), add_counts, jnp.zeros_like(counts))
    local_rank = jnp.sum((jnp.cumsum(hits, 0) - hits) * hits, 1)
    positions = jnp.sum(hits * (before + doc_offsets)[None, :], 1) + local_rank
    rope_keys = rotate(key_latent[:, LATENT:].astype(jnp.float32), positions).astype(jnp.bfloat16)
    key_rows = jnp.concatenate([key_latent[:, :LATENT], rope_keys], 1)
    block_keys, query_docs, query_positions, block_owners = (
        lax.all_gather(key_rows, "head", axis=0, tiled=True),
        lax.all_gather(doc_ids, "head", axis=0, tiled=True),
        lax.all_gather(positions, "head", axis=0, tiled=True),
        lax.all_gather(owners[:, 0], "head", axis=0, tiled=True),
    )
    tokens = q_nope.shape[0]
    slot_count = max(1, 2 * tokens // (n_ctx * n_head))
    outgoing = dispatch(
        block_owners, block_keys, n_ctx, lax.axis_index("head") * slot_count, slot_count
    )
    received = lax.all_to_all(outgoing, "ctx", split_axis=0, concat_axis=0, tiled=True)
    cache = received.reshape(n_ctx * slot_count, key_rows.shape[1])
    heads = w_key.shape[0]
    nope = q_nope.reshape(tokens, heads, NOPE)
    absorbed = jnp.einsum("thd,hdc->thc", nope, w_key, preferred_element_type=jnp.float32).astype(
        jnp.bfloat16
    )
    rotated = rotate(
        q_rope.reshape(tokens, heads, ROPE).astype(jnp.float32), query_positions[:, None]
    ).astype(jnp.bfloat16)
    query = jnp.concatenate([absorbed, rotated], 2)
    q_index = lax.axis_index("ctx") * tokens + jnp.arange(tokens, dtype=jnp.int32)
    scale = (NOPE + ROPE) ** (-0.5)
    highest = jnp.full((tokens, heads), -1e30, jnp.float32)
    rows = lax.all_gather(block_keys, "ctx", axis=0, tiled=True)
    docs = lax.all_gather(query_docs, "ctx", axis=0, tiled=True)
    k_index = jnp.arange(rows.shape[0], dtype=jnp.int32)
    mask = ((query_docs[:, None] == docs[None, :]) & (k_index[None, :] <= q_index[:, None]))[
        :, None, :
    ]
    scores = jnp.einsum("thc,kc->thk", query, rows, preferred_element_type=jnp.float32) * scale
    raised = jnp.maximum(highest, jnp.max(jnp.where(mask, scores, -1e30), 2))
    weights = jnp.where(mask, jnp.exp(scores - raised[..., None]), 0.0)
    total = jnp.sum(weights, 2)
    mixed = jnp.einsum(
        "thk,kc->thc",
        weights.astype(jnp.bfloat16),
        rows[:, :LATENT],
        preferred_element_type=jnp.float32,
    )
    latent_out = (mixed / total[..., None]).astype(jnp.bfloat16)
    attended = jnp.einsum(
        "thc,hcd->thd", latent_out, w_value, preferred_element_type=jnp.float32
    ).astype(jnp.bfloat16)
    return (attended.reshape(tokens, heads * VDIM), cache)


def solution(mesh):
    in_specs = (
        P("ctx", "head"),
        P("ctx", "head"),
        P(("ctx", "head"), None),
        P(("ctx", "head")),
        P(),
        P(("ctx", "head"), None),
        P("head", None, None),
        P("head", None, None),
    )
    out_specs = (P("ctx", "head"), P(("ctx", "head"), None))
    return jax.shard_map(local, mesh=mesh, in_specs=in_specs, out_specs=out_specs, check_vma=False)
```

profile of v0, /device:TPU:12, one launch (start us, length us, event | category | flops | bytes accessed | tf_op | source)
XLA Modules:
  0.0 298.4 jit_solution(7218796092261339773)
XLA Ops:
  7.2 0.8 fusion.41
  8.1 0.7 fusion.40
  8.8 0.7 slice_convert_fusion
  9.5 0.7 slice.23
  10.2 1.3 dynamic-slice
  11.5 0.2 dynamic-update-slice.1
  11.6 77.0 %all-reduce.1 = s32[1024]{0:T(1024)S(1)} all-reduce(s32[1024]{0:T(1024)S(1)} %dynamic-update-slice.1), channel_id=2, replica_groups=mesh['ctx'=32,'head'=8] {'ctx','head'}, use_global_device_ids=true, to_apply=%add.1 | all-reduce | flops 1024 | bytes 8192
  88.8 3.0 %while.10 = (s32[]{:T(128)}, s32[4]{0:T(128)S(1)}, s32[]{:T(128)}, s32[256,4]{1,0:T(8,128)S(1)}, s32[]{:T(128)}, /*index=5*/s32[]{:T(128)}, s32[]{:T(128)}) while((s32[]{:T(128)}, s32[4]{0:T(128)S(1)}, s32[]{:T(128)}, s32[256,4]{1,0:T(8,128)S(1)}, s32[]{:T(128)}, /*index=5*/s32[]{:T(128)}, s32[]{:T(128)}) %tuple.32), condition=%wide.region_2.3_spmd, body=%wide.region_1.2_spmd.sunk | while | flops 9 | bytes 171 | solution.py:20
  92.5 0.7 add.42
  93.2 0.8 select_reduce_fusion.1
  94.3 14.6 %all_gather.29 = bf16[128,576]{1,0:T(8,128)(2,1)S(1)} all-gather(bf16[16,576]{1,0:T(8,128)(2,1)S(1)} %pad_maximum_fusion), channel_id=1, replica_groups=mesh['ctx'=32,'head'=8] {'head'}, dimensions={0}, use_global_device_ids=true | all-gather | bytes 165888 | tf_op jit(solution)/shard_map/all_gather | solution.py:64
  109.0 0.8 copy.31
  109.8 0.9 dynamic-update-slice
  110.7 0.7 bitcast_dynamic-update-slice_fusion
  111.4 9.7 %all-reduce.4 = (s32[128]{0:T(128)S(1)}, s32[128]{0:T(128)S(1)}, s32[128]{0:T(128)S(1)}) all-reduce(s32[128]{0:T(128)S(1)} %get-tuple-element.53, s32[128]{0:T(128)S(1)} %dynamic-update-slice, s32[128]{0:T(128)S(1)} %bitcast_dynamic-update-slice_fusion), channel_id=1, replica_groups=mesh['ctx'=32,'head'=8] {'head'}, use_global_device_ids=true, to_apply=%add.2 | all-reduce | flops 384 | bytes 3072
  121.2 0.2 reduce_window_sum.23
  121.3 0.3 fusion.17
  121.6 0.5 broadcast.125
  122.1 0.7 reduce
  122.8 0.7 reshape.188
  123.5 14.3 %all-to-all-start = ((bf16[32,2,288]{2,1,0:T(2,128)(2,1)}), bf16[32,2,288]{2,1,0:T(2,128)(2,1)S(1)}, u32[]{:S(2)}, u32[]{:S(2)}) async-start(bf16[32,2,288]{2,1,0:T(2,128)(2,1)} %reshape.188), calls=%async_computation | async-start | bytes 98304 | tf_op jit(solution)/shard_map/all_to_all | solution.py:74
  137.9 1.0 copy.30
  138.9 65.0 %all-gather.2 = s32[32,1,128]{2,1,0:T(1,128)S(1)} all-gather(s32[1,1,128]{2,1,0:T(1,128)S(1)} %bitcast.46), channel_id=1, replica_groups=mesh['ctx'=32,'head'=8] {'ctx'}, dimensions={0}, use_global_device_ids=true | all-gather | bytes 16896 | tf_op jit(solution)/shard_map/all_gather | solution.py:89
  204.1 1.5 fusion.11
  205.5 0.5 fusion.10
  206.2 0.6 copy.47
  206.8 51.4 %all-gather.5.cloned.1.call-done = bf16[4096,576]{0,1:T(8,128)(2,1)} async-done(((bf16[128,576]{0,1:T(8,128)(2,1)}), bf16[4096,576]{0,1:T(8,128)(2,1)}) %all-gather.5.cloned.1.call-update) | async-done | bytes 4718608 | tf_op jit(solution)/shard_map/all_gather | solution.py:88
  258.2 10.0 %select_reduce_fusion = (f32[128,8]{0,1:T(8,128)S(1)}, f32[128,8,4096]{2,0,1:T(8,128)S(1)}) fusion(pred[128,4096]{1,0:T(8,128)(4,1)S(1)} %fusion.10, bf16[4096,576]{0,1:T(8,128)(2,1)} %all-gather.5.cloned.1.call-done, bf16[128,8,32]{0,2,1:T(8,128)(2,1)S(1)} %get-tuple-element.48, bf16[128,8,32]{0,2,1:T(8,128)(2,1)S(1)} %get-tuple-element.47, ...), kind=kOutput, calls=%fused_computation.2 | convolution fusion | flops 4847959040 | bytes 23203840 | tf_op jit(solution)/shard_map/thc,kc->thk/dot_general | solution.py:94
  268.3 5.7 %copy-done.1 = f32[128,8,4096]{2,0,1:T(8,128)} copy-done((f32[128,8,4096]{2,0,1:T(8,128)}, f32[128,8,4096]{2,0,1:T(8,128)S(1)}, u32[]{:S(2)}) %copy-start.1) | copy-done | bytes 16777240
  274.0 4.8 %fusion = f32[128,8]{0,1:T(8,128)S(1)} fusion(f32[128,8,4096]{2,0,1:T(8,128)S(1)} %get-tuple-element.56, f32[128,8]{0,1:T(8,128)S(1)} %broadcast_maximum_fusion, pred[128,4096]{1,0:T(8,128)(4,1)S(1)} %fusion.10), kind=kLoop, calls=%fused_computation.3 | loop fusion | flops 16776192 | bytes 17309696 | tf_op jit(solution)/shard_map/reduce_sum | solution.py:97
  278.8 11.9 %convolution_convert_fusion.1 = bf16[8,128,128]{1,2,0:T(8,128)(2,1)S(1)} fusion(bf16[8,512,128]{2,1,0:T(8,128)(2,1)S(1)} %copy-done.2, f32[128,8]{0,1:T(8,128)S(1)} %fusion, f32[128,8,4096]{2,0,1:T(8,128)} %copy-done.1, f32[128,8]{0,1:T(8,128)S(1)} %broadcast_maximum_fusion, pred[128,4096]{1,0:T(8,128)(4,1)S(1)} %fusion.10, ...), kind=kOutput, calls=%fused_computation.18 | convolution fusion | flops 4447141888 | bytes 22814720 | tf_op jit(solution)/shard_map/thc,hcd->thd/dot_general | solution.py:105
  290.7 0.9 copy.35
  (106 shorter events, 2.3 us)
Async XLA Ops:
  7.2 196.9 %copy-start = (bf16[8,128,512]{2,1,0:T(8,128)(2,1)S(1)}, bf16[8,128,512]{2,1,0:T(8,128)(2,1)}, u32[]{:S(2)}) copy-start(bf16[8,128,512]{2,1,0:T(8,128)(2,1)} %param.16) | copy-start | bytes 3145732
  7.2 251.1 %all-gather.5.cloned.1.call-start = ((), (), s32[]{:S(2)}) async-start(), calls=%async_computation.1 | async-start | bytes 4866048 | tf_op jit(solution)/shard_map/all_gather | solution.py:88
  123.5 82.5 %all-to-all-start = ((bf16[32,2,288]{2,1,0:T(2,128)(2,1)}), bf16[32,2,288]{2,1,0:T(2,128)(2,1)S(1)}, u32[]{:S(2)}, u32[]{:S(2)}) async-start(bf16[32,2,288]{2,1,0:T(2,128)(2,1)} %reshape.188), calls=%async_computation | async-start | bytes 98304 | tf_op jit(solution)/shard_map/all_to_all | solution.py:74
  268.3 5.7 %copy-start.1 = (f32[128,8,4096]{2,0,1:T(8,128)}, f32[128,8,4096]{2,0,1:T(8,128)S(1)}, u32[]{:S(2)}) copy-start(f32[128,8,4096]{2,0,1:T(8,128)S(1)} %get-tuple-element.56) | copy-start | bytes 50331652
  274.0 4.8 %copy-start.2 = (bf16[8,512,128]{2,1,0:T(8,128)(2,1)S(1)}, bf16[8,512,128]{2,1,0:T(8,128)(2,1)}, u32[]{:S(2)}) copy-start(bf16[8,512,128]{2,1,0:T(8,128)(2,1)} %param.17) | copy-start | bytes 3145732
Sparse Core Ops, SparseCore 0:
  109.9 148.2 all-gather.4
where the time goes:
time: 299 us; the launch traced here: 298 us
  blocking collectives  166 us (56%)
  waiting for transfers between devices  51.4 us (17%)
  matrix products  23.7 us (8%)
  between operations  14.9 us (5%)
  starting transfers between devices  14.4 us (5%)
  local copies, waits for them, and re-layouts  14.3 us (5%)
  other arithmetic  11.8 us (4%)
    unnamed x2, blocking collectives  86.7 us
    all_gather x1, blocking collectives, local(): docs = lax.all_gather(query_docs, 'ctx', axis=0, tiled=True)  65 us
    all_gather x1, waiting for transfers between devices, local(): rows = lax.all_gather(block_keys, 'ctx', axis=0, tiled=True)  51.4 us
    all_gather x1, blocking collectives, local(): lax.all_gather(key_rows, 'head', axis=0, tiled=True)  14.6 us
    all_to_all x1, starting transfers between devices, local(): lax.all_to_all(outgoing, 'ctx', split_axis=0, concat_axis=0, tiled=True)  14.3 us
    dot_general x1, matrix products, local(): jnp.einsum('thc,hcd->thd', latent_out, w_value, preferred_element_type=jn...  11.9 us
    unnamed x18, local copies, waits for them, and re-layouts  11.1 us
    dot_general x1, matrix products, local(): jnp.einsum('thc,kc->thk', query, rows, preferred_element_type=jnp.float32)  10 us
  transfers between devices with their start and end apart: 2, of which 1 were waited for; matrix products, arithmetic and copies ran while one was open for 3% of the time, Pallas kernels for 0%

commit v1 on v0

v1 whole, which is shorter than its diff:
```python
import functools

import jax
import jax.numpy as jnp
import numpy as np
from jax import lax
from jax.experimental import pallas as pl
from jax.experimental.pallas import tpu as pltpu
from jax.sharding import PartitionSpec as P

NOPE = 128
ROPE = 64
LATENT = 512
VDIM = 128
HEADS = 8
TOK = 128
HALF = 64
WIDE = 640
STRIP = 16
TILE = 256
BIG = float(2.0**100)
DEAD = -1e30
SCALE = (NOPE + ROPE) ** -0.5 * 1.4426950408889634
INVERSE = [float(v) for v in (10000.0 ** (-2.0 * np.arange(32) / 64.0)).astype(np.float32)]
DOC = 64
GONE = 68
NAT = 69
OWNER = 70
COUNT = 72
BLOCK = 80

MESH = pl.DeviceIdType.MESH
NT = (((1,), (1,)), ((), ()))
NN = (((1,), (0,)), ((), ()))


def iota(shape, dim):
    return lax.broadcasted_iota(jnp.int32, shape, dim)


def place(y, zl, x, zh, core):
    return (lax.rem(y, 4) * 8 + lax.rem(zl, 2) * 4 + lax.rem(x, 4), lax.rem(zh, 4) * 2 + core)


def inverse_lanes(shape):
    index = lax.rem(iota(shape, 1), 32)
    out = jnp.zeros(shape, jnp.float32)
    for j, value in enumerate(INVERSE):
        out = jnp.where(index == j, value, out)
    return out


def cos_sin(angle):
    turns = jnp.floor(angle * 0.6366197723675814 + 0.5)
    rest = angle - turns * 1.5703125
    rest = rest - turns * 4.837512969970703125e-4
    rest = rest - turns * 7.54978995489188216e-8
    z = rest * rest
    sine = rest + rest * z * (
        -1.6666654611e-1 + z * (8.3321608736e-3 - z * 1.9515295891e-4)
    )
    cosine = 1.0 - 0.5 * z + z * z * (
        4.166664568298827e-2 + z * (-1.388731625493765e-3 + z * 2.443315711809948e-5)
    )
    quadrant = turns.astype(jnp.int32) & 3
    swap = (quadrant & 1) == 1
    c = jnp.where(swap, sine, cosine)
    s = jnp.where(swap, cosine, sine)
    c = jnp.where((quadrant == 1) | (quadrant == 2), -c, c)
    s = jnp.where(quadrant >= 2, -s, s)
    return c, s


def turn(values, cosine, signed_sine):
    first = lax.rem(iota(values.shape, 1), 64) < 32
    partner = jnp.where(first, pltpu.roll(values, 96, 1), pltpu.roll(values, 32, 1))
    return values * cosine + partner * signed_sine


def sign_sine(sine):
    return jnp.where(lax.rem(iota(sine.shape, 1), 64) < 32, -sine, sine)


def nat_of(k):
    return lax.div(lax.rem(k, 64), 16) * 32 + lax.div(k, 64) * 16 + lax.rem(k, 16)


def kernel(
    qn_hbm, qr_hbm, kl_hbm, doc_ref, off_ref, own_hbm, wk_hbm, wv_hbm,
    out_ref, cache_ref,
    qn, qr, kl, own, wk, wv, raw, keys, query, acc, top, total, mask, cos_t, sin_t,
    s1, r1, s2, r2, hq_out, hq, hacc, htop, htotal, hout, hin,
    local_sem, pa_send, pa_recv, raw_send, raw_recv, m_send, m_recv, sib_send, sib_recv,
    c1_send, c1_recv, c2_send, c2_recv, h_send, h_recv,
):
    ctx = lax.axis_index("ctx")
    head = lax.axis_index("head")
    y, zl, x = lax.div(ctx, 8), lax.rem(lax.div(ctx, 4), 2), lax.rem(ctx, 4)
    zh, core = lax.div(head, 2), lax.rem(head, 2)
    odd = lax.rem(y, 2) == 1
    even = lax.rem(y, 2) == 0
    lane_group = zl * 4 + x

    z_up = lax.rem(zh * 2 + zl + 1, 8)
    z_down = lax.rem(zh * 2 + zl + 7, 8)
    to_z_up = place(y, lax.rem(z_up, 2), x, lax.div(z_up, 2), core)
    to_z_down = place(y, lax.rem(z_down, 2), x, lax.div(z_down, 2), core)
    to_x_up = place(y, zl, x + 1, zh, core)
    to_x_down = place(y, zl, x + 3, zh, core)
    to_y_up = place(y + 1, zl, x, zh, core)
    sibling = (ctx, zh * 2 + 1 - core)
    z_peers = [place(y, zl, x, zh + d, core) for d in (1, 2, 3)]
    y_peers = [place(y + d, zl, x, zh, core) for d in (1, 2, 3)]
    group_peers = []
    for d in range(1, 8):
        j = lax.rem(lane_group + d, 8)
        group_peers.append(place(y, lax.div(j, 4), lax.rem(j, 4), zh, core))
    other_zh = zh + zl * 2 + 3
    other_z = place(y, zl + 1, x, other_zh, core)

    locals_ = [
        pltpu.make_async_copy(kl_hbm, kl, local_sem.at[0]),
        pltpu.make_async_copy(own_hbm, own, local_sem.at[1]),
        pltpu.make_async_copy(qr_hbm, qr, local_sem.at[2]),
        pltpu.make_async_copy(qn_hbm, qn, local_sem.at[3]),
        pltpu.make_async_copy(wk_hbm, wk, local_sem.at[4]),
        pltpu.make_async_copy(wv_hbm, wv, local_sem.at[5]),
    ]
    for copy in locals_:
        copy.start()
    barrier = pltpu.get_barrier_semaphore()
    greeted = z_peers + y_peers + group_peers + [sibling, other_z]
    for peer in greeted:
        pl.semaphore_signal(barrier, inc=1, device_id=peer, device_id_type=MESH)

    lane128 = iota((TOK, 128), 1)

    @pl.when(even)
    def _():
        blank = jnp.where(iota((2 * HALF, 128), 1) == GONE, 1.0, 0.0).astype(jnp.bfloat16)
        blank = blank.reshape(2, HALF, 128)
        zero = jnp.zeros((2, HALF, LATENT), jnp.bfloat16)
        for s in (2, 6, 10, 14):
            keys[0, s : s + 2, :, :LATENT] = zero
            keys[0, s : s + 2, :, LATENT:] = blank
        for s in (8, 10, 12, 14):
            keys[1, s : s + 2, :, :LATENT] = zero
            keys[1, s : s + 2, :, LATENT:] = blank

    hq[TOK + STRIP :, :LATENT] = jnp.zeros((TOK - STRIP, LATENT), jnp.bfloat16)
    hq[TOK + STRIP :, LATENT:] = jnp.where(
        iota((TOK - STRIP, 128), 1) == GONE, 1.0, 0.0
    ).astype(jnp.bfloat16)
    inverse = inverse_lanes((8, 128))[0:1, :]
    token = (ctx * TOK + iota((TOK, 128), 0)).astype(jnp.float32)
    c, s = cos_sin(token * inverse)
    cos_t[...] = c
    sin_t[...] = sign_sine(s)
    for core_half in (0, 1):
        k = iota((TOK, 128), 1)
        dead = (k < 64) & (nat_of(core_half * 64 + lax.rem(k, 64)) > iota((TOK, 128), 0))
        mask[core_half] = jnp.where(dead, DEAD, 0.0)

    docs = jnp.zeros((STRIP, 128), jnp.int32)
    for r in range(STRIP):
        docs = jnp.where(iota((STRIP, 128), 0) == r, doc_ref[r], docs)
    lane = iota((STRIP, 128), 1)
    locals_[0].wait()
    locals_[1].wait()
    facts = jnp.where((lane == DOC + docs) | (lane == COUNT + docs), 1.0, 0.0)
    facts = jnp.where(lane == BLOCK + lax.rem(ctx, 16), 1.0, facts)
    facts = jnp.where(lane == NAT, (head * STRIP + iota((STRIP, 128), 0)).astype(jnp.float32), facts)
    facts = jnp.where(lane == OWNER, own[...].astype(jnp.float32), facts)
    mine = pl.ds(pl.multiple_of(zh * STRIP, STRIP), STRIP)
    raw[core, mine, :LATENT] = kl[:, :LATENT]
    raw[core, mine, LATENT:] = jnp.concatenate(
        [kl[:, LATENT:], facts[:, ROPE:].astype(jnp.bfloat16)], 1
    )
    pl.semaphore_wait(barrier, len(greeted))

    pa = [
        pltpu.make_async_remote_copy(
            src_ref=raw.at[core, mine], dst_ref=raw.at[core, mine],
            send_sem=pa_send.at[d], recv_sem=pa_recv.at[d],
            device_id=z_peers[d], device_id_type=MESH,
        )
        for d in range(3)
    ]
    for copy in pa:
        copy.start()

    locals_[2].wait()
    for pair in range(4):
        v = turn(qr[:, pair * 128 : pair * 128 + 128].astype(jnp.float32), cos_t[...], sin_t[...])
        base = pair * 2 * TOK
        query[base : base + TOK, LATENT:] = v.astype(jnp.bfloat16)
        query[base + TOK : base + 2 * TOK, LATENT:] = pltpu.roll(v, 64, 1).astype(jnp.bfloat16)
    locals_[3].wait()
    locals_[4].wait()
    for h in range(HEADS):
        a = lax.dot_general(
            qn[:, h * NOPE : (h + 1) * NOPE], wk[h], NN, preferred_element_type=jnp.float32
        )
        query[h * TOK : (h + 1) * TOK, :LATENT] = a.astype(jnp.bfloat16)

    plan = {0: [], 1: []}

    def send(scheme, src, dst, to, sem, half=None):
        a, b = keys.at[scheme, src], keys.at[scheme, dst]
        if half is not None:
            a, b = a.at[pl.ds(half * 32, 32)], b.at[pl.ds(half * 32, 32)]
        return pltpu.make_async_remote_copy(
            src_ref=a, dst_ref=b, send_sem=m_send.at[sem],
            recv_sem=m_recv.at[16 if half == 1 else dst], device_id=to, device_id_type=MESH,
        )

    def go(scheme, src, dst, to, half=None, cond=None, inside=None):
        number = len(plan[scheme])
        make = functools.partial(send, scheme, src, dst, to, number, half)
        plan[scheme].append((make, cond if inside is None else inside))
        if cond is None:
            make().start()
        else:
            @pl.when(cond)
            def _():
                make().start()

    def arrived(scheme, slot, half=None):
        ref = keys.at[scheme, slot]
        sem = slot
        if half is not None:
            ref = ref.at[pl.ds(half * 32, 32)]
            sem = 16 if half == 1 else slot
        pltpu.make_async_copy(ref, ref, m_recv.at[sem]).wait()

    def share(scheme, slot):
        return pltpu.make_async_remote_copy(
            src_ref=keys.at[scheme, slot], dst_ref=keys.at[scheme, slot],
            send_sem=sib_send.at[slot], recv_sem=sib_recv.at[slot],
            device_id=sibling, device_id_type=MESH,
        )

    def own_slot(half):
        v = raw[half, :, LATENT:].astype(jnp.float32)
        cc = jnp.concatenate([cos_t[n * 32 + half * 16 : n * 32 + half * 16 + 16, :] for n in range(4)], 0)
        ss = jnp.concatenate([sin_t[n * 32 + half * 16 : n * 32 + half * 16 + 16, :] for n in range(4)], 0)
        rotated = jnp.where(iota((HALF, 128), 1) < ROPE, turn(v, cc, ss), v)
        keys[half, 0, :, :LATENT] = raw[half, :, :LATENT]
        keys[half, 0, :, LATENT:] = rotated.astype(jnp.bfloat16)

    for d in range(3):
        pa[d].wait_recv()
    share_raw = pltpu.make_async_remote_copy(
        src_ref=raw.at[core], dst_ref=raw.at[core], send_sem=raw_send, recv_sem=raw_recv,
        device_id=sibling, device_id_type=MESH,
    )
    share_raw.start()

    on_a, on_b = core == 0, core == 1

    @pl.when(on_a)
    def _():
        own_slot(0)
        go(0, 0, 4, to_x_up)
        go(0, 0, 8, to_x_down)
        go(0, 0, 1, to_z_up)
        go(0, 0, 2, to_y_up, cond=even)

    @pl.when(on_b)
    def _():
        own_slot(1)
        go(1, 0, 1, to_x_up)
        go(1, 0, 2, to_x_down)
        go(1, 0, 4, to_z_up)
        go(1, 0, 8, to_y_up, cond=even)

    pltpu.make_async_copy(raw.at[1 - core], raw.at[1 - core], raw_recv).wait()

    @pl.when(on_a)
    def _():
        own_slot(1)

    @pl.when(on_b)
    def _():
        own_slot(0)

    bound = jnp.where(
        (lane128 == GONE)
        | ((lane128 >= BLOCK) & (lane128 < BLOCK + 16) & (lane128 - BLOCK > lax.rem(ctx, 16))),
        -BIG,
        0.0,
    )
    hot = jnp.concatenate(
        [raw[n % 2, (n // 2) * 16 : (n // 2) * 16 + 16, LATENT:] for n in range(8)], 0
    ).astype(jnp.float32)
    bound = jnp.where((lane128 >= DOC) & (lane128 < DOC + 4), (hot - 1.0) * BIG, bound)
    bound = bound.astype(jnp.bfloat16)
    for h in range(HEADS):
        rows = slice(h * TOK, (h + 1) * TOK)
        query[rows, LATENT:] = jnp.where(lane128 < ROPE, query[rows, LATENT:], bound)

    asks, helps = ctx == 16, ctx == 8

    def ask():
        return pltpu.make_async_remote_copy(
            src_ref=hq_out, dst_ref=hq.at[pl.ds(0, TOK + STRIP)],
            send_sem=h_send.at[0], recv_sem=h_recv.at[0], device_id=place(1, zl, x, zh, core),
            device_id_type=MESH,
        )

    def answer():
        return pltpu.make_async_remote_copy(
            src_ref=hout, dst_ref=hin, send_sem=h_send.at[1], recv_sem=h_recv.at[1],
            device_id=place(2, zl, x, zh, core), device_id_type=MESH,
        )

    @pl.when(asks)
    def _():
        for h in range(HEADS):
            hq_out[h * 16 : (h + 1) * 16, :] = query[h * TOK : h * TOK + 16, :]
        part = hq_out[:TOK, LATENT:]
        hq_out[:TOK, LATENT:] = jnp.where(lane128 >= BLOCK, jnp.zeros_like(part), part)
        hq_out[TOK:, :] = keys[0, 0, 0:STRIP, :]
        ask().start()

    both = raw[...].reshape(TOK, WIDE)
    pick = jnp.where(iota((8, 128), 1) == OWNER, 1.0, 0.0).astype(jnp.bfloat16)
    owner = lax.dot_general(pick, both[:, LATENT:], NT, preferred_element_type=jnp.float32)[0:1, :]
    line = iota((64, TOK), 0)
    named = jnp.where(lax.rem(line, 16) < 8, lax.div(line, 16) * 8 + lax.rem(line, 16), -1)
    hits = owner == named.astype(jnp.float32)
    hits_b = jnp.where(hits, 1.0, 0.0).astype(jnp.bfloat16)
    before = nat_of(iota((TOK, TOK), 0)) < nat_of(iota((TOK, TOK), 1))
    rank = lax.dot_general(
        hits_b, jnp.where(before, 1.0, 0.0).astype(jnp.bfloat16), NN,
        preferred_element_type=jnp.float32,
    )
    chosen = jnp.where(hits & (rank == head.astype(jnp.float32)), 1.0, 0.0).astype(jnp.bfloat16)
    rows64 = lax.dot_general(chosen, both, NN, preferred_element_type=jnp.float32)
    counts = lax.dot_general(
        jnp.ones((64, TOK), jnp.bfloat16), both[:, LATENT:], NN, preferred_element_type=jnp.float32
    )
    lane64 = iota((64, 128), 1)
    s1[:, :LATENT] = rows64[:, :LATENT].astype(jnp.bfloat16)
    s1[:, LATENT:] = jnp.where(
        (lane64 >= COUNT) & (lane64 < COUNT + 4), counts, rows64[:, LATENT:]
    ).astype(jnp.bfloat16)
    my_y = pl.ds(pl.multiple_of(y * 16, 16), 16)
    r1[my_y, :] = s1[my_y, :]

    def cache1(d):
        there = lax.rem(y + d, 4)
        return pltpu.make_async_remote_copy(
            src_ref=s1.at[pl.ds(pl.multiple_of(there * 16, 16), 16)], dst_ref=r1.at[my_y],
            send_sem=c1_send.at[d - 1], recv_sem=c1_recv.at[d - 1], device_id=y_peers[d - 1],
            device_id_type=MESH,
        )

    for d in (1, 2, 3):
        cache1(d).start()

    my_group = pl.ds(pl.multiple_of(lane_group * 16, 16), 16)

    def cache2(d):
        there = lax.rem(lane_group + d, 8)
        return pltpu.make_async_remote_copy(
            src_ref=s2.at[pl.ds(pl.multiple_of(there * 16, 16), 16)], dst_ref=r2.at[my_group],
            send_sem=c2_send.at[d - 1], recv_sem=c2_recv.at[d - 1], device_id=group_peers[d - 1],
            device_id_type=MESH,
        )

    def cache_middle():
        for d in (1, 2, 3):
            cache1(d).wait_recv()
        to, source = iota((128, 64), 0), iota((128, 64), 1)
        ys, j = lax.rem(to, 16), lax.div(to, 16)
        permute = jnp.where((ys < 4) & (source == ys * 16 + j), 1.0, 0.0).astype(jnp.bfloat16)
        s2[...] = lax.dot_general(
            permute, r1[...], NN, preferred_element_type=jnp.float32
        ).astype(jnp.bfloat16)
        r2[my_group, :] = s2[my_group, :]
        for d in range(1, 8):
            cache2(d).start()

    def cache_end():
        for d in range(1, 8):
            cache2(d).wait_recv()
        slot, source = iota((32, 128), 0), iota((32, 128), 1)
        permute = jnp.where(
            source == lax.rem(slot, 8) * 16 + lax.div(slot, 8), 1.0, 0.0
        ).astype(jnp.bfloat16)
        rows = lax.dot_general(permute, r2[...], NN, preferred_element_type=jnp.float32)
        facts = rows[:, LATENT:]
        lane32 = iota((32, 128), 1)
        sums = jnp.sum(facts, 0, keepdims=True)
        lane1 = iota((1, 128), 1)

        def lane_of(values, index, at):
            return jnp.sum(jnp.where(at == index, values, 0.0), 1, keepdims=True)

        number = sum(d * lane_of(facts, DOC + d, lane32) for d in (1, 2, 3))
        start = sum(
            jnp.where(number > d, lane_of(sums, COUNT + d, lane1), 0.0) for d in range(3)
        )
        offset = jnp.zeros((32, 1), jnp.float32)
        for d in range(4):
            offset = jnp.where(number == d, off_ref[d].astype(jnp.float32), offset)
        at = (iota((32, 1), 0) * TOK).astype(jnp.float32) + lane_of(facts, NAT, lane32)
        c, s = cos_sin((offset + at - start) * inverse)
        turned = turn(facts, c, sign_sine(s))
        cache_ref[:, :LATENT] = rows[:, :LATENT].astype(jnp.bfloat16)
        cache_ref[:, LATENT:] = turned[:, :ROPE].astype(jnp.bfloat16)

    def a_near():
        @pl.when(on_a)
        def _():
            arrived(0, 1)
            go(0, 1, 5, to_x_up)
            go(0, 1, 9, to_x_down)
            share(0, 1).start()

            @pl.when(odd)
            def _():
                arrived(0, 2)
                go(0, 2, 6, to_x_up, inside=odd)
                go(0, 2, 10, to_x_down, inside=odd)
                go(0, 2, 3, to_z_down, inside=odd)
                share(0, 2).start()
                arrived(0, 3)
                go(0, 3, 7, to_x_up, inside=odd)
                go(0, 3, 11, to_x_down, inside=odd)
                share(0, 3).start()

    def b_near():
        @pl.when(on_b)
        def _():
            arrived(1, 1)
            go(1, 1, 3, to_x_up, half=0)
            go(1, 1, 5, to_z_up)
            go(1, 1, 9, to_y_up, cond=even)
            share(1, 1).start()
            arrived(1, 2)
            go(1, 2, 3, to_x_down, half=1)
            go(1, 2, 6, to_z_down)
            go(1, 2, 10, to_y_up, cond=even)
            share(1, 2).start()
            arrived(1, 3, half=0)
            arrived(1, 3, half=1)
            go(1, 3, 7, to_z_down)
            go(1, 3, 11, to_y_up, cond=even)
            share(1, 3).start()

    def a_far(g):
        def step():
            arrived(0, 4 + g)
            if g in (0, 3):
                go(0, 4 + g, 12 + g, to_x_up, inside=None if g < 2 else odd)
            share(0, 4 + g).start()
            arrived(0, 8 + g)
            if g in (1, 2):
                go(0, 8 + g, 12 + g, to_x_down, inside=None if g < 2 else odd)
            share(0, 8 + g).start()

        pl.when(on_a if g < 2 else on_a & odd)(step)

    def b_far(k):
        @pl.when(on_b & odd)
        def _():
            arrived(1, 8 + k)
            go(1, 8 + k, 12 + k, to_z_up if k < 2 else to_z_down, inside=odd)
            share(1, 8 + k).start()

        @pl.when(on_b)
        def _():
            arrived(1, 4 + k)
            share(1, 4 + k).start()

    def last(k):
        @pl.when(on_a if k < 2 else on_a & odd)
        def _():
            arrived(0, 12 + k)
            share(0, 12 + k).start()

        @pl.when(on_b & odd)
        def _():
            arrived(1, 12 + k)
            share(1, 12 + k).start()

    def shared(chunk):
        for i in range(4):
            slot = chunk * 4 + i
            if slot == 0:
                continue

            @pl.when(on_a if chunk < 2 else on_a & odd)
            def _():
                share(1, slot).wait_recv()

            @pl.when(on_b if i < 2 else on_b & odd)
            def _():
                share(0, slot).wait_recv()

    def scores(chunk, rows, ref):
        q = ref[rows, :]
        out = []
        for scheme in (0, 1):
            k = keys[scheme, chunk * 4 : chunk * 4 + 4].reshape(4 * HALF, WIDE)
            out.append(lax.dot_general(q, k, NT, preferred_element_type=jnp.float32) * SCALE)
        return out

    def absorb(parts, values, rows, first, acc, top, total):
        size = rows.stop - rows.start
        most = jnp.max(functools.reduce(jnp.maximum, parts), 1, keepdims=True)
        if not first:
            old = top[rows, 0:1]
            most = jnp.maximum(old, most)
            shrink = jnp.exp2(old - most)
        weights = [jnp.exp2(p - most) for p in parts]
        added = sum(
            w[:, n * 128 : (n + 1) * 128] for w in weights for n in range(w.shape[1] // 128)
        )
        top[rows, :] = jnp.broadcast_to(most, (size, 128))
        total[rows, :] = added if first else total[rows, :] * shrink + added
        mixed = None
        for w, v in zip(weights, values):
            d = lax.dot_general(w.astype(jnp.bfloat16), v, NN, preferred_element_type=jnp.float32)
            mixed = d if mixed is None else mixed + d
        acc[rows, :] = mixed if first else acc[rows, :] * shrink + mixed

    def latents(chunk):
        return [
            keys[scheme, chunk * 4 : chunk * 4 + 4, :, :LATENT].reshape(4 * HALF, LATENT)
            for scheme in (0, 1)
        ]

    tiles = [slice(i * TILE, (i + 1) * TILE) for i in range(HEADS * TOK // TILE)]

    def tile(chunk, i, parts):
        if chunk == 0:
            masked = []
            for scheme in (0, 1):
                p = parts[scheme]
                own_part = (p[:, :128].reshape(TILE // TOK, TOK, 128) + mask[scheme][None]).reshape(
                    TILE, 128
                )
                masked.append(jnp.concatenate([own_part, p[:, 128:]], 1))
            parts = masked
        absorb(parts, latents(chunk), tiles[i], chunk == 0, acc, top, total)

    all_h = slice(0, TOK)

    def help_first():
        ask().wait_recv()
        strip = hq[TOK:, :]
        p = lax.dot_general(hq[:TOK, :], strip, NT, preferred_element_type=jnp.float32) * SCALE
        p = jnp.where(lane128 <= lax.rem(iota((TOK, 128), 0), 16), p, DEAD)
        absorb([p], [strip[:, :LATENT]], all_h, True, hacc, htop, htotal)

    def help_chunk(chunk):
        absorb(scores(chunk, all_h, hq), latents(chunk), all_h, False, hacc, htop, htotal)

    def help_last():
        hout[...] = (hacc[...] / jnp.sum(htotal[...], 1, keepdims=True)).astype(jnp.bfloat16)
        answer().start()

    a_near()
    b_near()
    shared(0)

    @pl.when(helps)
    def _():
        help_first()
        help_chunk(0)

    parts = scores(0, tiles[0], query)
    for chunk in range(4):
        for i in range(4):
            following = scores(chunk, tiles[i + 1], query) if i < 3 else None
            tile(chunk, i, parts)
            parts = following
            if chunk == 0:
                a_far(i)
                b_far(i)
            if chunk == 1:
                if i == 0:
                    cache_middle()
            if chunk == 2:
                last(i)
        if chunk < 3:
            shared(chunk + 1)

            @pl.when(helps)
            def _():
                help_chunk(chunk + 1)
                if chunk == 2:
                    help_last()

            parts = scores(chunk + 1, tiles[0], query)
        if chunk == 2:
            cache_end()

    @pl.when(asks)
    def _():
        answer().wait_recv()

    locals_[5].wait()
    spare = iota((TOK, LATENT), 0) < 8
    for h in range(HEADS):
        rows = slice(h * TOK, (h + 1) * TOK)
        latent = (acc[rows, :] / jnp.sum(total[rows, :], 1, keepdims=True)).astype(jnp.bfloat16)
        theirs = jnp.concatenate(
            [hin[h * 16 : (h + 1) * 16, :], jnp.zeros((TOK - 16, LATENT), jnp.bfloat16)], 0
        )
        latent = jnp.where(spare & asks, theirs, latent)
        out_ref[:, h * VDIM : (h + 1) * VDIM] = lax.dot_general(
            latent, wv[h], NN, preferred_element_type=jnp.float32
        ).astype(jnp.bfloat16)

    for copy in pa:
        copy.wait_send()
    share_raw.wait_send()
    for scheme, on in ((0, on_a), (1, on_b)):
        @pl.when(on)
        def _():
            for make, cond in plan[scheme]:
                if cond is None:
                    make().wait_send()
                else:
                    @pl.when(cond)
                    def _():
                        make().wait_send()
            for slot in range(1, 16):
                g = slot % 4 if scheme == 0 else slot // 4
                if g < 2:
                    share(scheme, slot).wait_send()
                else:
                    @pl.when(odd)
                    def _():
                        share(scheme, slot).wait_send()
    for d in (1, 2, 3):
        cache1(d).wait_send()
    for d in range(1, 8):
        cache2(d).wait_send()

    @pl.when(asks)
    def _():
        ask().wait_send()

    @pl.when(helps)
    def _():
        answer().wait_send()


def local(q_nope, q_rope, key_latent, doc_ids, doc_offsets, owners, w_key, w_value):
    bf, f32 = jnp.bfloat16, jnp.float32
    vmem = pltpu.VMEM
    dma = pltpu.SemaphoreType.DMA
    hbm = pl.BlockSpec(memory_space=pl.ANY)
    smem = pl.BlockSpec(memory_space=pltpu.SMEM)
    rows = HEADS * TOK
    return pl.pallas_call(
        kernel,
        out_shape=(
            jax.ShapeDtypeStruct((TOK, HEADS * VDIM), bf),
            jax.ShapeDtypeStruct((32, LATENT + ROPE), bf),
        ),
        in_specs=[hbm, hbm, hbm, smem, smem, hbm, hbm, hbm],
        out_specs=(pl.BlockSpec(memory_space=vmem), pl.BlockSpec(memory_space=vmem)),
        scratch_shapes=[
            vmem((TOK, HEADS * NOPE), bf),
            vmem((TOK, HEADS * ROPE), bf),
            vmem((STRIP, LATENT + ROPE), bf),
            vmem((STRIP, 1), jnp.int32),
            vmem((HEADS, NOPE, LATENT), bf),
            vmem((HEADS, LATENT, VDIM), bf),
            vmem((2, HALF, WIDE), bf),
            vmem((2, 16, HALF, WIDE), bf),
            vmem((rows, WIDE), bf),
            vmem((rows, LATENT), f32),
            vmem((rows, 128), f32),
            vmem((rows, 128), f32),
            vmem((2, TOK, 128), f32),
            vmem((TOK, 128), f32),
            vmem((TOK, 128), f32),
            vmem((64, WIDE), bf),
            vmem((64, WIDE), bf),
            vmem((128, WIDE), bf),
            vmem((128, WIDE), bf),
            vmem((TOK + STRIP, WIDE), bf),
            vmem((2 * TOK, WIDE), bf),
            vmem((TOK, LATENT), f32),
            vmem((TOK, 128), f32),
            vmem((TOK, 128), f32),
            vmem((TOK, LATENT), bf),
            vmem((TOK, LATENT), bf),
            dma((6,)),
            dma((3,)),
            dma((3,)),
            dma,
            dma,
            dma((24,)),
            dma((17,)),
            dma((16,)),
            dma((16,)),
            dma((3,)),
            dma((3,)),
            dma((7,)),
            dma((7,)),
            dma((2,)),
            dma((2,)),
        ],
        compiler_params=pltpu.CompilerParams(
            collective_id=0, has_side_effects=True, vmem_limit_bytes=48 * 2**20
        ),
        name="latent_attention",
    )(q_nope, q_rope, key_latent, doc_ids, doc_offsets, owners, w_key, w_value)


def solution(mesh):
    in_specs = (
        P("ctx", "head"),
        P("ctx", "head"),
        P(("ctx", "head"), None),
        P(("ctx", "head")),
        P(),
        P(("ctx", "head"), None),
        P("head", None, None),
        P("head", None, None),
    )
    out_specs = (P("ctx", "head"), P(("ctx", "head"), None))
    return jax.shard_map(local, mesh=mesh, in_specs=in_specs, out_specs=out_specs, check_vma=False)
```

time: 299 us -> 49 us (0.16)
  the two profiles are of different devices: /device:TPU:12 before, /device:TPU:17 now
where the time goes in v1:
time: 49 us; the launch traced here: 48.7 us
  Pallas kernels  40.9 us (83%)
  local copies, waits for them, and re-layouts  7.1 us (14%)
  between operations  0.66 us (1%)
    pallas_call x1, Pallas kernels, local(): pl.pallas_call(kernel, out_shape=(jax.ShapeDtypeStruct((TOK, HEADS * VDIM...  40.9 us
    unnamed x17, local copies, waits for them, and re-layouts  7.1 us

profile of v1, /device:TPU:17, one launch (start us, length us, event | category | flops | bytes accessed | tf_op | source)
XLA Modules:
  0.0 48.7 jit_solution(15110404406978104094)
XLA Ops:
  0.6 0.0 copy-start.6
  0.6 0.0 copy-start.5
  0.7 0.7 %copy.10.own_hbm = s32[16,1]{1,0:T(8,128)S(1)} copy(s32[16,1]{0,1:T(1,128)} %param.13) | data formatting | bytes 128 | tf_op args[5]
  1.4 0.0 copy-done.6
  1.4 0.0 copy-done.5
  1.4 0.0 copy-start
  1.4 1.2 %copy-done = bf16[8,128,512]{2,1,0:T(8,128)(2,1)S(1)} copy-done((bf16[8,128,512]{2,1,0:T(8,128)(2,1)S(1)}, bf16[8,128,512]{2,1,0:T(8,128)(2,1)}, u32[]{:S(2)}) %copy-start) | copy-done | bytes 1048600
  2.6 0.0 copy-start.1
  2.6 1.2 %copy-done.1 = bf16[8,512,128]{2,1,0:T(8,128)(2,1)S(1)} copy-done((bf16[8,512,128]{2,1,0:T(8,128)(2,1)S(1)}, bf16[8,512,128]{2,1,0:T(8,128)(2,1)}, u32[]{:S(2)}) %copy-start.1) | copy-done | bytes 1048600
  3.9 0.0 copy-start.2
  3.9 0.9 %copy-done.2 = bf16[128,1024]{1,0:T(8,128)(2,1)S(1)} copy-done((bf16[128,1024]{1,0:T(8,128)(2,1)S(1)}, bf16[128,1024]{1,0:T(8,128)(2,1)}, u32[]{:S(2)}) %copy-start.2) | copy-done | bytes 262168
  4.8 0.0 copy-start.3
  4.8 0.9 %copy-done.3 = bf16[128,512]{1,0:T(8,128)(2,1)S(1)} copy-done((bf16[128,512]{1,0:T(8,128)(2,1)S(1)}, bf16[128,512]{1,0:T(8,128)(2,1)}, u32[]{:S(2)}) %copy-start.3) | copy-done | bytes 131096
  5.7 0.0 copy-start.4
  5.7 0.7 %copy-done.4 = bf16[16,576]{1,0:T(8,128)(2,1)S(1)} copy-done((bf16[16,576]{1,0:T(8,128)(2,1)S(1)}, bf16[16,576]{1,0:T(8,128)(2,1)}, u32[]{:S(2)}) %copy-start.4) | copy-done | bytes 18456
  6.4 40.9 %latent_attention.1 = (bf16[128,1024]{1,0:T(8,128)(2,1)S(1)}, bf16[32,576]{1,0:T(8,128)(2,1)S(1)}) custom-call(bf16[128,1024]{1,0:T(8,128)(2,1)S(1)} %copy-done.2, bf16[128,512]{1,0:T(8,128)(2,1)S(1)} %copy-done.3, bf16[16,576]{1,0:T(8,128)(2,1)S(1)} %copy-done.4, s32[16]{0:T(128)S(1)} %copy-done.5, s32[4]{0:T(128)S(1)} %copy-done.6, ...), custom_call_target="tpu_custom_call" | custom-call | tf_op jit(solution)/shard_map/latent_attention/pallas_call | solution.py:661
  47.4 0.7 %copy.13 = bf16[128,1024]{1,0:T(8,128)(2,1)} copy(bf16[128,1024]{1,0:T(8,128)(2,1)S(1)} %get-tuple-element.4) | data formatting | bytes 524288
  48.1 0.6 %copy.14 = bf16[32,576]{1,0:T(8,128)(2,1)} copy(bf16[32,576]{1,0:T(8,128)(2,1)S(1)} %get-tuple-element.5) | data formatting | bytes 73728
Async XLA Ops:
  0.6 0.8 %copy-start.6 = (s32[4]{0:T(128)S(1)}, s32[4]{0:T(128)}, u32[]{:S(2)}) copy-start(s32[4]{0:T(128)} %off_ref.1) | copy-start | bytes 52
  0.6 0.8 %copy-start.5 = (s32[16]{0:T(128)S(1)}, s32[16]{0:T(128)}, u32[]{:S(2)}) copy-start(s32[16]{0:T(128)} %doc_ref.1) | copy-start | bytes 196
  1.4 1.2 %copy-start = (bf16[8,128,512]{2,1,0:T(8,128)(2,1)S(1)}, bf16[8,128,512]{2,1,0:T(8,128)(2,1)}, u32[]{:S(2)}) copy-start(bf16[8,128,512]{2,1,0:T(8,128)(2,1)} %wk_hbm.1) | copy-start | bytes 3145732
  2.6 1.2 %copy-start.1 = (bf16[8,512,128]{2,1,0:T(8,128)(2,1)S(1)}, bf16[8,512,128]{2,1,0:T(8,128)(2,1)}, u32[]{:S(2)}) copy-start(bf16[8,512,128]{2,1,0:T(8,128)(2,1)} %wv_hbm.1) | copy-start | bytes 3145732
  3.9 0.9 %copy-start.2 = (bf16[128,1024]{1,0:T(8,128)(2,1)S(1)}, bf16[128,1024]{1,0:T(8,128)(2,1)}, u32[]{:S(2)}) copy-start(bf16[128,1024]{1,0:T(8,128)(2,1)} %qn_hbm.1) | copy-start | bytes 786436
  4.8 0.9 %copy-start.3 = (bf16[128,512]{1,0:T(8,128)(2,1)S(1)}, bf16[128,512]{1,0:T(8,128)(2,1)}, u32[]{:S(2)}) copy-start(bf16[128,512]{1,0:T(8,128)(2,1)} %qr_hbm.1) | copy-start | bytes 393220
  5.7 0.7 %copy-start.4 = (bf16[16,576]{1,0:T(8,128)(2,1)S(1)}, bf16[16,576]{1,0:T(8,128)(2,1)}, u32[]{:S(2)}) copy-start(bf16[16,576]{1,0:T(8,128)(2,1)} %kl_hbm.1) | copy-start | bytes 55300

commit v2 on v1

v2 whole, which is shorter than its diff:
```python
import functools

import jax
import jax.numpy as jnp
import numpy as np
from jax import lax
from jax.experimental import pallas as pl
from jax.experimental.pallas import tpu as pltpu
from jax.sharding import PartitionSpec as P

NOPE = 128
ROPE = 64
LATENT = 512
VDIM = 128
HEADS = 8
TOK = 128
HALF = 64
WIDE = 640
STRIP = 16
TILE = 256
BIG = float(2.0**100)
DEAD = -1e30
SCALE = (NOPE + ROPE) ** -0.5 * 1.4426950408889634
INVERSE = [float(v) for v in (10000.0 ** (-2.0 * np.arange(32) / 64.0)).astype(np.float32)]
DOC = 64
GONE = 68
NAT = 69
OWNER = 70
COUNT = 72
BLOCK = 80
EXTRA = 64

ORDER = (
    (0, 0), (0, 1), (1, 0), (2, 0), (0, 2), (0, 3), (3, 0), (1, 1),
    (2, 1), (3, 1), (1, 2), (2, 2), (3, 2), (1, 3), (2, 3), (3, 3),
)
CHUNKS = ((0, 2), (2, 6), (6, 10), (10, 14), (14, 16))

MESH = pl.DeviceIdType.MESH
NT = (((1,), (1,)), ((), ()))
NN = (((1,), (0,)), ((), ()))


def iota(shape, dim):
    return lax.broadcasted_iota(jnp.int32, shape, dim)


def place(y, zl, x, zh, core):
    return (lax.rem(y, 4) * 8 + lax.rem(zl, 2) * 4 + lax.rem(x, 4), lax.rem(zh, 4) * 2 + core)


def inverse_lanes(shape):
    index = lax.rem(iota(shape, 1), 32)
    out = jnp.zeros(shape, jnp.float32)
    for j, value in enumerate(INVERSE):
        out = jnp.where(index == j, value, out)
    return out


def cos_sin(angle):
    turns = jnp.floor(angle * 0.6366197723675814 + 0.5)
    rest = angle - turns * 1.5703125
    rest = rest - turns * 4.837512969970703125e-4
    rest = rest - turns * 7.54978995489188216e-8
    z = rest * rest
    sine = rest + rest * z * (
        -1.6666654611e-1 + z * (8.3321608736e-3 - z * 1.9515295891e-4)
    )
    cosine = 1.0 - 0.5 * z + z * z * (
        4.166664568298827e-2 + z * (-1.388731625493765e-3 + z * 2.443315711809948e-5)
    )
    quadrant = turns.astype(jnp.int32) & 3
    swap = (quadrant & 1) == 1
    c = jnp.where(swap, sine, cosine)
    s = jnp.where(swap, cosine, sine)
    c = jnp.where((quadrant == 1) | (quadrant == 2), -c, c)
    s = jnp.where(quadrant >= 2, -s, s)
    return c, s


def turn(values, cosine, signed_sine):
    first = lax.rem(iota(values.shape, 1), 64) < 32
    partner = jnp.where(first, pltpu.roll(values, 96, 1), pltpu.roll(values, 32, 1))
    return values * cosine + partner * signed_sine


def sign_sine(sine):
    return jnp.where(lax.rem(iota(sine.shape, 1), 64) < 32, -sine, sine)


def nat_of(k):
    return lax.div(lax.rem(k, 64), 16) * 32 + lax.div(k, 64) * 16 + lax.rem(k, 16)


def kernel(
    qn_hbm, qr_hbm, kl_hbm, doc_ref, off_ref, own_ref, wk_hbm, wv_hbm,
    out_hbm, cache_ref,
    qn, qr, kl, wk, wv, raw, keys, query, acc, top, total, mask, cos_t, sin_t, cos_p, sin_p, raw_p,
    s1, r1, s2, r2, strip, hq_out, hout, hin, out_v,
    local_sem, pa_send, pa_recv, raw_send, raw_recv, m_send, m_recv, sib_send, sib_recv,
    c1_send, c1_recv, c2_send, c2_recv, h_send, h_recv,
):
    ctx = lax.axis_index("ctx")
    head = lax.axis_index("head")
    y, zl, x = lax.div(ctx, 8), lax.rem(lax.div(ctx, 4), 2), lax.rem(ctx, 4)
    zh, core = lax.div(head, 2), lax.rem(head, 2)
    odd = lax.rem(y, 2) == 1
    even = lax.rem(y, 2) == 0
    lane_group = zl * 4 + x

    z_up = lax.rem(zh * 2 + zl + 1, 8)
    z_down = lax.rem(zh * 2 + zl + 7, 8)
    to_z_up = place(y, lax.rem(z_up, 2), x, lax.div(z_up, 2), core)
    to_z_down = place(y, lax.rem(z_down, 2), x, lax.div(z_down, 2), core)
    to_x_up = place(y, zl, x + 1, zh, core)
    to_x_down = place(y, zl, x + 3, zh, core)
    to_x_across = place(y, zl, x + 2, zh, core)
    to_y_up = place(y + 1, zl, x, zh, core)
    sibling = (ctx, zh * 2 + 1 - core)
    z_peers = []
    for d in range(1, 8):
        z = lax.rem(zh * 2 + zl + d, 8)
        z_peers.append(place(y, lax.rem(z, 2), x, lax.div(z, 2), core))
    y_peers = [place(y + d, zl, x, zh, core) for d in (1, 2, 3)]
    group_peers = []
    for d in range(1, 8):
        j = lax.rem(lane_group + d, 8)
        group_peers.append(place(y, lax.div(j, 4), lax.rem(j, 4), zh, core))
    barrier = pltpu.get_barrier_semaphore()
    greeted = z_peers + y_peers + group_peers[:3] + group_peers[4:] + [sibling]
    for peer in greeted:
        pl.semaphore_signal(barrier, inc=1, device_id=peer, device_id_type=MESH)

    locals_ = [
        pltpu.make_async_copy(kl_hbm, kl, local_sem.at[0]),
        pltpu.make_async_copy(qr_hbm, qr, local_sem.at[1]),
        pltpu.make_async_copy(qn_hbm, qn, local_sem.at[2]),
        pltpu.make_async_copy(wk_hbm, wk, local_sem.at[3]),
        pltpu.make_async_copy(wv_hbm, wv, local_sem.at[4]),
    ]
    for copy in locals_:
        copy.start()
    lane128 = iota((TOK, 128), 1)

    @pl.when(even)
    def _():
        blank = jnp.where(iota((HALF, 128), 1) == GONE, 1.0, 0.0).astype(jnp.bfloat16)
        zero = jnp.zeros((HALF, LATENT), jnp.bfloat16)
        for scheme in (0, 1):
            for pos, (_, g) in enumerate(ORDER):
                if g >= 2:
                    keys[pos, scheme, :, :LATENT] = zero
                    keys[pos, scheme, :, LATENT:] = blank

    @pl.when(ctx != 8)
    def _():
        query[HEADS * TOK :, :] = jnp.zeros((EXTRA, WIDE), jnp.bfloat16)

    top[HEADS * TOK :, :] = jnp.zeros((EXTRA, 128), jnp.float32)
    total[HEADS * TOK :, :] = jnp.zeros((EXTRA, 128), jnp.float32)
    acc[HEADS * TOK :, :] = jnp.zeros((EXTRA, LATENT), jnp.float32)
    rest = TOK - STRIP
    strip[STRIP:, :LATENT] = jnp.zeros((rest, LATENT), jnp.bfloat16)
    strip[STRIP:, LATENT:] = jnp.where(iota((rest, 128), 1) == GONE, 1.0, 0.0).astype(jnp.bfloat16)
    inverse = inverse_lanes((8, 128))[0:1, :]
    token = (ctx * TOK + iota((TOK, 128), 0)).astype(jnp.float32)
    c, s = cos_sin(token * inverse)
    cos_t[...] = c
    sin_t[...] = sign_sine(s)
    other = y * 8 + (1 - zl) * 4 + x
    k = iota((HALF, 128), 0)
    at = other * TOK + lax.div(k, 16) * 32 + core * 16 + lax.rem(k, 16)
    c, s = cos_sin(at.astype(jnp.float32) * inverse)
    cos_p[...] = c
    sin_p[...] = sign_sine(s)
    mask[...] = jnp.where(nat_of(lane128) > iota((TOK, 128), 0), DEAD, 0.0)

    docs = jnp.zeros((STRIP, 128), jnp.int32)
    owners = docs
    for r in range(STRIP):
        docs = jnp.where(iota((STRIP, 128), 0) == r, doc_ref[r], docs)
        owners = jnp.where(iota((STRIP, 128), 0) == r, own_ref[r], owners)
    lane = iota((STRIP, 128), 1)
    locals_[0].wait()
    facts = jnp.where((lane == DOC + docs) | (lane == COUNT + docs), 1.0, 0.0)
    facts = jnp.where(lane == BLOCK + lax.rem(ctx, 16), 1.0, facts)
    facts = jnp.where(lane == NAT, (head * STRIP + iota((STRIP, 128), 0)).astype(jnp.float32), facts)
    facts = jnp.where(lane == OWNER, owners.astype(jnp.float32), facts)
    mine = pl.ds(pl.multiple_of(zh * STRIP, STRIP), STRIP)
    raw[core, mine, :LATENT] = kl[:, :LATENT]
    raw[core, mine, LATENT:] = jnp.concatenate(
        [kl[:, LATENT:], facts[:, ROPE:].astype(jnp.bfloat16)], 1
    )
    pl.semaphore_wait(barrier, len(greeted))

    pa = [
        pltpu.make_async_remote_copy(
            src_ref=raw.at[core, mine],
            dst_ref=raw.at[core, mine] if d % 2 == 0 else raw_p.at[mine],
            send_sem=pa_send.at[d - 1], recv_sem=pa_recv.at[d - 1],
            device_id=z_peers[d - 1], device_id_type=MESH,
        )
        for d in range(1, 8)
    ]
    for d in (4, 2, 6, 3, 5, 1, 7):
        pa[d - 1].start()

    locals_[1].wait()
    for pair in range(4):
        v = turn(qr[:, pair * 128 : pair * 128 + 128].astype(jnp.float32), cos_t[...], sin_t[...])
        base = pair * 2 * TOK
        query[base : base + TOK, LATENT:] = v.astype(jnp.bfloat16)
        query[base + TOK : base + 2 * TOK, LATENT:] = pltpu.roll(v, 64, 1).astype(jnp.bfloat16)
    locals_[2].wait()
    locals_[3].wait()
    for h in range(HEADS):
        a = lax.dot_general(
            qn[:, h * NOPE : (h + 1) * NOPE], wk[h], NN, preferred_element_type=jnp.float32
        )
        query[h * TOK : (h + 1) * TOK, :LATENT] = a.astype(jnp.bfloat16)

    plan = {0: {}, 1: {}}

    def send(scheme, src, dst, to, sem):
        return pltpu.make_async_remote_copy(
            src_ref=keys.at[src, scheme], dst_ref=keys.at[dst, scheme],
            send_sem=m_send.at[sem], recv_sem=m_recv.at[dst], device_id=to, device_id_type=MESH,
        )

    def go(scheme, src, dst, to, cond=None, inside=None):
        src, dst = ORDER.index(src), ORDER.index(dst)
        make = functools.partial(send, scheme, src, dst, to, len(plan[scheme]))
        plan[scheme][src, dst, cond is None] = (make, cond if inside is None else inside)
        if cond is None:
            make().start()
        else:
            @pl.when(cond)
            def _():
                make().start()

    def arrived(scheme, pos):
        ref = keys.at[pos, scheme]
        pltpu.make_async_copy(ref, ref, m_recv.at[pos]).wait()

    def share(scheme, pos):
        return pltpu.make_async_remote_copy(
            src_ref=keys.at[pos, scheme], dst_ref=keys.at[pos, scheme],
            send_sem=sib_send.at[pos], recv_sem=sib_recv.at[pos],
            device_id=sibling, device_id_type=MESH,
        )

    def fill(scheme, pos, rows, cc, ss):
        v = rows[:, LATENT:].astype(jnp.float32)
        rotated = jnp.where(iota((HALF, 128), 1) < ROPE, turn(v, cc, ss), v)
        keys[pos, scheme, :, :LATENT] = rows[:, :LATENT]
        keys[pos, scheme, :, LATENT:] = rotated.astype(jnp.bfloat16)

    def own_slot(half):
        cc = jnp.concatenate([cos_t[n * 32 + half * 16 : n * 32 + half * 16 + 16, :] for n in range(4)], 0)
        ss = jnp.concatenate([sin_t[n * 32 + half * 16 : n * 32 + half * 16 + 16, :] for n in range(4)], 0)
        fill(half, 0, raw[half], cc, ss)

    for d in (2, 4, 6):
        pa[d - 1].wait_recv()
    share_raw = pltpu.make_async_remote_copy(
        src_ref=raw.at[core], dst_ref=raw.at[core], send_sem=raw_send, recv_sem=raw_recv,
        device_id=sibling, device_id_type=MESH,
    )
    share_raw.start()

    on_a, on_b = core == 0, core == 1

    @pl.when(on_a)
    def _():
        own_slot(0)
        go(0, (0, 0), (0, 2), to_y_up, cond=even)

    @pl.when(on_b)
    def _():
        own_slot(1)
        go(1, (0, 0), (1, 0), to_x_up)
        go(1, (0, 0), (2, 0), to_x_down)
        go(1, (0, 0), (3, 0), to_x_across)

    for d in (1, 3, 5, 7):
        pa[d - 1].wait_recv()

    @pl.when(on_a)
    def _():
        fill(0, 1, raw_p[...], cos_p[...], sin_p[...])
        go(0, (0, 1), (0, 3), to_y_up, cond=even)
        go(0, (0, 0), (1, 0), to_x_up)
        go(0, (0, 0), (2, 0), to_x_down)
        go(0, (0, 0), (3, 0), to_x_across)
        share(0, 1).start()

    @pl.when(on_b)
    def _():
        fill(1, 1, raw_p[...], cos_p[...], sin_p[...])
        go(1, (0, 0), (0, 2), to_y_up, cond=even)
        go(1, (0, 1), (0, 3), to_y_up, cond=even)
        share(1, 1).start()

    pltpu.make_async_copy(raw.at[1 - core], raw.at[1 - core], raw_recv).wait()

    @pl.when(on_a)
    def _():
        own_slot(1)

    @pl.when(on_b)
    def _():
        own_slot(0)

    bound = jnp.where(
        (lane128 == GONE)
        | ((lane128 >= BLOCK) & (lane128 < BLOCK + 16) & (lane128 - BLOCK > lax.rem(ctx, 16))),
        -BIG,
        0.0,
    )
    hot = jnp.concatenate(
        [raw[n % 2, (n // 2) * 16 : (n // 2) * 16 + 16, LATENT:] for n in range(8)], 0
    ).astype(jnp.float32)
    bound = jnp.where((lane128 >= DOC) & (lane128 < DOC + 4), (hot - 1.0) * BIG, bound)
    bound = bound.astype(jnp.bfloat16)
    for h in range(HEADS):
        rows = slice(h * TOK, (h + 1) * TOK)
        query[rows, LATENT:] = jnp.where(lane128 < ROPE, query[rows, LATENT:], bound)

    asks, helps = ctx == 16, ctx == 8

    extra = slice(HEADS * TOK, HEADS * TOK + EXTRA)

    def ask(part):
        return pltpu.make_async_remote_copy(
            src_ref=hq_out.at[pl.ds(0, EXTRA) if part == 0 else pl.ds(EXTRA, STRIP)],
            dst_ref=query.at[pl.ds(HEADS * TOK, EXTRA)] if part == 0 else strip.at[pl.ds(0, STRIP)],
            send_sem=h_send.at[part], recv_sem=h_recv.at[part],
            device_id=place(1, zl, x, zh, core), device_id_type=MESH,
        )

    def answer():
        return pltpu.make_async_remote_copy(
            src_ref=hout, dst_ref=hin, send_sem=h_send.at[2], recv_sem=h_recv.at[2],
            device_id=place(2, zl, x, zh, core), device_id_type=MESH,
        )

    @pl.when(asks)
    def _():
        firsts = jnp.concatenate(
            [query[h * TOK : h * TOK + 16, :].astype(jnp.float32)[:8] for h in range(HEADS)], 0
        )
        firsts = jnp.where(iota((EXTRA, WIDE), 1) >= LATENT + BLOCK, 0.0, firsts)
        hq_out[:EXTRA, :] = firsts.astype(jnp.bfloat16)
        hq_out[EXTRA:, :] = keys[0, 0, 0:STRIP, :]
        ask(0).start()
        ask(1).start()

    my_y = pl.ds(pl.multiple_of(y * 16, 16), 16)

    def cache1(d):
        there = lax.rem(y + d, 4)
        return pltpu.make_async_remote_copy(
            src_ref=s1.at[pl.ds(pl.multiple_of(there * 16, 16), 16)], dst_ref=r1.at[my_y],
            send_sem=c1_send.at[d - 1], recv_sem=c1_recv.at[d - 1], device_id=y_peers[d - 1],
            device_id_type=MESH,
        )

    def cache_begin():
        both = raw[...].reshape(TOK, WIDE)
        pick = jnp.where(iota((8, 128), 1) == OWNER, 1.0, 0.0).astype(jnp.bfloat16)
        owner = lax.dot_general(pick, both[:, LATENT:], NT, preferred_element_type=jnp.float32)[0:1, :]
        line = iota((64, TOK), 0)
        named = jnp.where(lax.rem(line, 16) < 8, lax.div(line, 16) * 8 + lax.rem(line, 16), -1)
        hits = owner == named.astype(jnp.float32)
        hits_b = jnp.where(hits, 1.0, 0.0).astype(jnp.bfloat16)
        before = nat_of(iota((TOK, TOK), 0)) < nat_of(iota((TOK, TOK), 1))
        rank = lax.dot_general(
            hits_b, jnp.where(before, 1.0, 0.0).astype(jnp.bfloat16), NN,
            preferred_element_type=jnp.float32,
        )
        chosen = jnp.where(hits & (rank == head.astype(jnp.float32)), 1.0, 0.0).astype(jnp.bfloat16)
        rows64 = lax.dot_general(chosen, both, NN, preferred_element_type=jnp.float32)
        counts = lax.dot_general(
            jnp.ones((64, TOK), jnp.bfloat16), both[:, LATENT:], NN, preferred_element_type=jnp.float32
        )
        lane64 = iota((64, 128), 1)
        s1[:, :LATENT] = rows64[:, :LATENT].astype(jnp.bfloat16)
        s1[:, LATENT:] = jnp.where(
            (lane64 >= COUNT) & (lane64 < COUNT + 4), counts, rows64[:, LATENT:]
        ).astype(jnp.bfloat16)
        r1[my_y, :] = s1[my_y, :]
        for d in (1, 2, 3):
            cache1(d).start()

    my_group = pl.ds(pl.multiple_of(lane_group * 16, 16), 16)

    def cache2(d):
        there = lax.rem(lane_group + d, 8)
        return pltpu.make_async_remote_copy(
            src_ref=s2.at[pl.ds(pl.multiple_of(there * 16, 16), 16)], dst_ref=r2.at[my_group],
            send_sem=c2_send.at[d - 1], recv_sem=c2_recv.at[d - 1], device_id=group_peers[d - 1],
            device_id_type=MESH,
        )

    def cache_middle():
        for d in (1, 2, 3):
            cache1(d).wait_recv()
        to, source = iota((128, 64), 0), iota((128, 64), 1)
        ys, j = lax.rem(to, 16), lax.div(to, 16)
        permute = jnp.where((ys < 4) & (source == ys * 16 + j), 1.0, 0.0).astype(jnp.bfloat16)
        s2[...] = lax.dot_general(
            permute, r1[...], NN, preferred_element_type=jnp.float32
        ).astype(jnp.bfloat16)
        r2[my_group, :] = s2[my_group, :]
        for d in range(1, 8):
            cache2(d).start()

    def cache_end():
        for d in range(1, 8):
            cache2(d).wait_recv()
        slot, source = iota((32, 128), 0), iota((32, 128), 1)
        permute = jnp.where(
            source == lax.rem(slot, 8) * 16 + lax.div(slot, 8), 1.0, 0.0
        ).astype(jnp.bfloat16)
        rows = lax.dot_general(permute, r2[...], NN, preferred_element_type=jnp.float32)
        facts = rows[:, LATENT:]
        lane32 = iota((32, 128), 1)
        sums = jnp.sum(facts, 0, keepdims=True)
        lane1 = iota((1, 128), 1)

        def lane_of(values, index, at):
            return jnp.sum(jnp.where(at == index, values, 0.0), 1, keepdims=True)

        number = sum(d * lane_of(facts, DOC + d, lane32) for d in (1, 2, 3))
        start = sum(
            jnp.where(number > d, lane_of(sums, COUNT + d, lane1), 0.0) for d in range(3)
        )
        offset = jnp.zeros((32, 1), jnp.float32)
        for d in range(4):
            offset = jnp.where(number == d, off_ref[d].astype(jnp.float32), offset)
        at = (iota((32, 1), 0) * TOK).astype(jnp.float32) + lane_of(facts, NAT, lane32)
        c, s = cos_sin((offset + at - start) * inverse)
        turned = turn(facts, c, sign_sine(s))
        cache_ref[:, :LATENT] = rows[:, :LATENT].astype(jnp.bfloat16)
        cache_ref[:, LATENT:] = turned.astype(jnp.bfloat16)

    def step(pos):
        xr, g = here = ORDER[pos]
        inside = None if g < 2 else odd

        @pl.when(on_a if g < 2 else on_a & odd)
        def _():
            arrived(0, pos)
            if xr == 0:
                go(0, here, (1, g), to_x_up, inside=inside)
                go(0, here, (2, g), to_x_down, inside=inside)
                go(0, here, (3, g), to_x_across, inside=inside)
            if g == 0:
                go(0, here, (xr, 1), to_z_up if xr == 1 else to_z_down)
            share(0, pos).start()

        @pl.when(on_b if g < 2 else on_b & odd)
        def _():
            arrived(1, pos)
            if g == 0:
                go(1, here, (xr, 2), to_y_up, cond=even)
                go(1, here, (xr, 1), to_z_down if xr == 2 else to_z_up)
            if g == 2 and xr > 0:
                go(1, here, (xr, 3), to_z_up if xr == 1 else to_z_down, inside=odd)
            share(1, pos).start()

    def shared(chunk):
        for pos in range(*CHUNKS[chunk]):
            if pos == 0:
                continue

            @pl.when(on_a if ORDER[pos][1] < 2 else on_a & odd)
            def _():
                share(1, pos).wait_recv()

            @pl.when(on_b if ORDER[pos][1] < 2 else on_b & odd)
            def _():
                share(0, pos).wait_recv()

    def rows_of(chunk):
        first, end = CHUNKS[chunk]
        return keys[first:end].reshape((end - first) * TOK, WIDE)

    def scores(q, k):
        return lax.dot_general(q, k, NT, preferred_element_type=jnp.float32) * SCALE

    def absorb(p, values, rows, first):
        size = rows.stop - rows.start
        most = jnp.max(p, 1, keepdims=True)
        if not first:
            old = top[rows, 0:1]
            most = jnp.maximum(old, most)
            shrink = jnp.exp2(old - most)
        weights = jnp.exp2(p - most)
        added = sum(weights[:, n * 128 : (n + 1) * 128] for n in range(p.shape[1] // 128))
        top[rows, :] = jnp.broadcast_to(most, (size, 128))
        total[rows, :] = added if first else total[rows, :] * shrink + added
        mixed = lax.dot_general(
            weights.astype(jnp.bfloat16), values, NN, preferred_element_type=jnp.float32
        )
        acc[rows, :] = mixed if first else acc[rows, :] * shrink + mixed

    count = HEADS * TOK // TILE
    tiles = [slice(i * TILE, (i + 1) * TILE) for i in range(count)]
    wide_tiles = tiles[:-1] + [slice(tiles[-1].start, extra.stop)]

    def tile(chunk, rows, p):
        if chunk == 0:
            own_part = p[:, :TOK].reshape(TILE // TOK, TOK, TOK) + mask[...][None]
            p = jnp.concatenate([own_part.reshape(TILE, TOK), p[:, TOK:]], 1)
        absorb(p, rows_of(chunk)[:, :LATENT], rows, chunk == 0)

    def sweep(chunk, order, after_first=None):
        p = scores(query[order[0], :], rows_of(chunk))
        for i, rows in enumerate(order):
            following = None
            if i + 1 < len(order):
                following = scores(query[order[i + 1], :], rows_of(chunk))
            tile(chunk, rows, p)
            p = following
            if i == 0 and after_first is not None:
                after_first()

    def help_first():
        ask(0).wait_recv()
        ask(1).wait_recv()
        p = scores(query[extra, :], strip[...])
        p = jnp.where(iota((EXTRA, TOK), 1) <= lax.rem(iota((EXTRA, TOK), 0), 8), p, DEAD)
        absorb(p, strip[:, :LATENT], extra, True)
        absorb(scores(query[extra, :], rows_of(0)), rows_of(0)[:, :LATENT], extra, False)

    def help_last():
        hout[...] = (acc[extra, :] / jnp.sum(total[extra, :], 1, keepdims=True)).astype(
            jnp.bfloat16
        )
        answer().start()

    cache_begin()
    shared(0)
    sweep(0, tiles)
    for pos in range(2, 6):
        step(pos)

    @pl.when(helps)
    def _():
        help_first()

    cache_middle()
    shared(1)
    sweep(1, wide_tiles)
    for pos in range(6, 13):
        step(pos)
    shared(2)

    @pl.when(helps)
    def _():
        sweep(2, [extra])

    @pl.when(jnp.logical_not(helps))
    def _():
        sweep(2, tiles)

    step(13)
    shared(3)
    sweep(3, wide_tiles)
    step(14)
    step(15)
    cache_end()
    shared(4)
    sweep(4, wide_tiles[::-1], lambda: pl.when(helps)(help_last))

    @pl.when(asks)
    def _():
        answer().wait_recv()
        theirs = hin[...].astype(jnp.float32)
        for h in range(HEADS):
            rows = slice(h * TOK, h * TOK + 8)
            acc[rows, :] = theirs[h * 8 : (h + 1) * 8]
            total[rows, :] = jnp.where(iota((8, 128), 1) == 0, 1.0, 0.0)

    locals_[4].wait()

    def store(part):
        columns = pl.ds(part * 4 * VDIM, 4 * VDIM)
        return pltpu.make_async_copy(
            out_v.at[:, columns], out_hbm.at[:, columns], local_sem.at[part]
        )

    for h in range(HEADS):
        rows = slice(h * TOK, (h + 1) * TOK)
        share_of = 1.0 / jnp.sum(total[rows, :], 1, keepdims=True)
        latent = (acc[rows, :] * share_of).astype(jnp.bfloat16)
        out_v[:, h * VDIM : (h + 1) * VDIM] = lax.dot_general(
            latent, wv[h], NN, preferred_element_type=jnp.float32
        ).astype(jnp.bfloat16)
        if h % 4 == 3:
            store(h // 4).start()

    store(0).wait()
    store(1).wait()
    for copy in pa:
        copy.wait_send()
    share_raw.wait_send()
    for scheme, on in ((0, on_a), (1, on_b)):
        @pl.when(on)
        def _():
            for make, cond in plan[scheme].values():
                if cond is None:
                    make().wait_send()
                else:
                    @pl.when(cond)
                    def _():
                        make().wait_send()
            for pos in range(1, 16):
                if ORDER[pos][1] < 2:
                    share(scheme, pos).wait_send()
                else:
                    @pl.when(odd)
                    def _():
                        share(scheme, pos).wait_send()
    for d in (1, 2, 3):
        cache1(d).wait_send()
    for d in range(1, 8):
        cache2(d).wait_send()

    @pl.when(asks)
    def _():
        ask(0).wait_send()
        ask(1).wait_send()

    @pl.when(helps)
    def _():
        answer().wait_send()


def local(q_nope, q_rope, key_latent, doc_ids, doc_offsets, owners, w_key, w_value):
    bf, f32 = jnp.bfloat16, jnp.float32
    vmem = pltpu.VMEM
    dma = pltpu.SemaphoreType.DMA
    hbm = pl.BlockSpec(memory_space=pl.ANY)
    smem = pl.BlockSpec(memory_space=pltpu.SMEM)
    rows = HEADS * TOK
    attended, cache = pl.pallas_call(
        kernel,
        out_shape=(
            jax.ShapeDtypeStruct((TOK, HEADS * VDIM), bf),
            jax.ShapeDtypeStruct((32, WIDE), bf),
        ),
        in_specs=[hbm, hbm, hbm, smem, smem, smem, hbm, hbm],
        out_specs=(hbm, pl.BlockSpec(memory_space=vmem)),
        scratch_shapes=[
            vmem((TOK, HEADS * NOPE), bf),
            vmem((TOK, HEADS * ROPE), bf),
            vmem((STRIP, LATENT + ROPE), bf),
            vmem((HEADS, NOPE, LATENT), bf),
            vmem((HEADS, LATENT, VDIM), bf),
            vmem((2, HALF, WIDE), bf),
            vmem((16, 2, HALF, WIDE), bf),
            vmem((rows + EXTRA, WIDE), bf),
            vmem((rows + EXTRA, LATENT), f32),
            vmem((rows + EXTRA, 128), f32),
            vmem((rows + EXTRA, 128), f32),
            vmem((TOK, 128), f32),
            vmem((TOK, 128), f32),
            vmem((TOK, 128), f32),
            vmem((HALF, 128), f32),
            vmem((HALF, 128), f32),
            vmem((HALF, WIDE), bf),
            vmem((64, WIDE), bf),
            vmem((64, WIDE), bf),
            vmem((128, WIDE), bf),
            vmem((128, WIDE), bf),
            vmem((TOK, WIDE), bf),
            vmem((EXTRA + STRIP, WIDE), bf),
            vmem((EXTRA, LATENT), bf),
            vmem((EXTRA, LATENT), bf),
            vmem((TOK, HEADS * VDIM), bf),
            dma((5,)),
            dma((7,)),
            dma((7,)),
            dma,
            dma,
            dma((24,)),
            dma((16,)),
            dma((16,)),
            dma((16,)),
            dma((3,)),
            dma((3,)),
            dma((7,)),
            dma((7,)),
            dma((3,)),
            dma((3,)),
        ],
        compiler_params=pltpu.CompilerParams(
            collective_id=0, has_side_effects=True, vmem_limit_bytes=60 * 2**20
        ),
        name="latent_attention",
    )(q_nope, q_rope, key_latent, doc_ids, doc_offsets, owners.reshape(STRIP), w_key, w_value)
    return attended, cache[:, : LATENT + ROPE]


def solution(mesh):
    in_specs = (
        P("ctx", "head"),
        P("ctx", "head"),
        P(("ctx", "head"), None),
        P(("ctx", "head")),
        P(),
        P(("ctx", "head"), None),
        P("head", None, None),
        P("head", None, None),
    )
    out_specs = (P("ctx", "head"), P(("ctx", "head"), None))
    return jax.shard_map(local, mesh=mesh, in_specs=in_specs, out_specs=out_specs, check_vma=False)
```

time: 49 us -> 42.9 us (0.88)
  local copies, waits for them, and re-layouts: 7.1 us -> 2.3 us
  Pallas kernels: 40.9 us -> 39.8 us
    unnamed x17 -> x4, local copies, waits for them, and re-layouts: 7.1 us -> 2.3 us
    pallas_call x1, Pallas kernels: 40.9 us -> 39.8 us  [local(): pl.pallas_call(kernel, out_shape=(jax.ShapeDtypeStruct((TOK, HEADS * VDIM...]
where the time goes in v2:
time: 42.9 us; the launch traced here: 42.8 us
  Pallas kernels  39.8 us (93%)
  local copies, waits for them, and re-layouts  2.3 us (5%)
  between operations  0.65 us (2%)
    pallas_call x1, Pallas kernels, local(): pl.pallas_call(kernel, out_shape=(jax.ShapeDtypeStruct((TOK, HEADS * VDIM...  39.8 us
    unnamed x4, local copies, waits for them, and re-layouts  2.3 us

profile of v2, /device:TPU:17, one launch (start us, length us, event | category | flops | bytes accessed | tf_op | source)
XLA Modules:
  0.0 42.8 jit_solution(3897933868935577813)
XLA Ops:
  0.6 39.8 %latent_attention.1 = (bf16[128,1024]{1,0:T(8,128)(2,1)}, bf16[32,640]{1,0:T(8,128)(2,1)}) custom-call(bf16[128,1024]{1,0:T(8,128)(2,1)} %qn_hbm.1, bf16[128,512]{1,0:T(8,128)(2,1)} %qr_hbm.1, bf16[16,576]{1,0:T(8,128)(2,1)} %kl_hbm.1, s32[16]{0:T(128)} %doc_ref.1, s32[4]{0:T(128)} %off_ref.1, s32[16]{0:T(128)} %bitcast.3, bf16[8,128,512]{2,1,0:T(8,128)(2,1)} %wk_hbm.1, ...), custom_call_target="tpu_custom_call" | custom-call | tf_op jit(solution)/shard_map/latent_attention/pallas_call | solution.py:648
  40.5 0.0 copy-start
  40.5 1.7 %copy.12 = bf16[128,1024]{1,0:T(8,128)(2,1)} copy(bf16[128,1024]{1,0:T(8,128)(2,1)} %get-tuple-element.8) | data formatting | bytes 524288
  42.1 0.0 copy-done
  42.1 0.6 %copy.13 = bf16[32,576]{1,0:T(8,128)(2,1)} copy(bf16[32,576]{1,0:T(8,128)(2,1)S(1)} %bitcast.2) | data formatting | bytes 73728
Async XLA Ops:
  40.5 1.7 %copy-start = (bf16[32,640]{1,0:T(8,128)(2,1)S(1)}, bf16[32,640]{1,0:T(8,128)(2,1)}, u32[]{:S(2)}) copy-start(bf16[32,640]{1,0:T(8,128)(2,1)} %get-tuple-element.5) | copy-start | bytes 122884

commit v3 on v2

--- a/solution.py
+++ b/solution.py
@@ -93,9 +93,9 @@
 
 
 def kernel(
-    qn_hbm, qr_hbm, kl_hbm, doc_ref, off_ref, own_ref, wk_hbm, wv_hbm,
+    qn_hbm, qr_hbm, kl_hbm, doc_hbm, off_hbm, own_hbm, wk_hbm, wv_hbm,
     out_hbm, cache_ref,
-    qn, qr, kl, wk, wv, raw, keys, query, acc, top, total, mask, cos_t, sin_t, cos_p, sin_p, raw_p,
+    qn, qr, kl, doc_ref, off_ref, own_ref, wk, wv, raw, keys, query, acc, top, total, mask, cos_t, sin_t, cos_p, sin_p, raw_p,
     s1, r1, s2, r2, strip, hq_out, hout, hin, out_v,
     local_sem, pa_send, pa_recv, raw_send, raw_recv, m_send, m_recv, sib_send, sib_recv,
     c1_send, c1_recv, c2_send, c2_recv, h_send, h_recv,
@@ -137,9 +137,12 @@
         pltpu.make_async_copy(qn_hbm, qn, local_sem.at[2]),
         pltpu.make_async_copy(wk_hbm, wk, local_sem.at[3]),
         pltpu.make_async_copy(wv_hbm, wv, local_sem.at[4]),
+        pltpu.make_async_copy(doc_hbm, doc_ref, local_sem.at[5]),
+        pltpu.make_async_copy(own_hbm, own_ref, local_sem.at[6]),
+        pltpu.make_async_copy(off_hbm, off_ref, local_sem.at[7]),
     ]
-    for copy in locals_:
-        copy.start()
+    for number in (5, 6, 0, 7, 1, 2, 3, 4):
+        locals_[number].start()
     lane128 = iota((TOK, 128), 1)
 
     @pl.when(even)
@@ -175,6 +178,8 @@
     sin_p[...] = sign_sine(s)
     mask[...] = jnp.where(nat_of(lane128) > iota((TOK, 128), 0), DEAD, 0.0)
 
+    for number in (5, 6, 7):
+        locals_[number].wait()
     docs = jnp.zeros((STRIP, 128), jnp.int32)
     owners = docs
     for r in range(STRIP):
@@ -643,20 +648,27 @@
     vmem = pltpu.VMEM
     dma = pltpu.SemaphoreType.DMA
     hbm = pl.BlockSpec(memory_space=pl.ANY)
-    smem = pl.BlockSpec(memory_space=pltpu.SMEM)
+    smem = pltpu.SMEM
     rows = HEADS * TOK
+    operands = (
+        q_nope, q_rope, key_latent, doc_ids, doc_offsets, owners.reshape(STRIP), w_key, w_value
+    )
+    operands = [pltpu.with_memory_space_constraint(a, pltpu.HBM) for a in operands]
     attended, cache = pl.pallas_call(
         kernel,
         out_shape=(
             jax.ShapeDtypeStruct((TOK, HEADS * VDIM), bf),
             jax.ShapeDtypeStruct((32, WIDE), bf),
         ),
-        in_specs=[hbm, hbm, hbm, smem, smem, smem, hbm, hbm],
+        in_specs=[hbm] * 8,
         out_specs=(hbm, pl.BlockSpec(memory_space=vmem)),
         scratch_shapes=[
             vmem((TOK, HEADS * NOPE), bf),
             vmem((TOK, HEADS * ROPE), bf),
             vmem((STRIP, LATENT + ROPE), bf),
+            smem((STRIP,), jnp.int32),
+            smem((4,), jnp.int32),
+            smem((STRIP,), jnp.int32),
             vmem((HEADS, NOPE, LATENT), bf),
             vmem((HEADS, LATENT, VDIM), bf),
             vmem((2, HALF, WIDE), bf),
@@ -680,7 +692,7 @@
             vmem((EXTRA, LATENT), bf),
             vmem((EXTRA, LATENT), bf),
             vmem((TOK, HEADS * VDIM), bf),
-            dma((5,)),
+            dma((8,)),
             dma((7,)),
             dma((7,)),
             dma,
@@ -697,10 +709,10 @@
             dma((3,)),
         ],
         compiler_params=pltpu.CompilerParams(
-            collective_id=0, has_side_effects=True, vmem_limit_bytes=60 * 2**20
+            collective_id=0, has_side_effects=True, vmem_limit_bytes=40 * 2**20
         ),
         name="latent_attention",
-    )(q_nope, q_rope, key_latent, doc_ids, doc_offsets, owners.reshape(STRIP), w_key, w_value)
+    )(*operands)
     return attended, cache[:, : LATENT + ROPE]
 
 

time: 42.9 us -> 40.2 us (0.937)
  Pallas kernels: 39.8 us -> 38.2 us
  local copies, waits for them, and re-layouts: 2.3 us -> 1.32 us
    pallas_call x1, Pallas kernels: 39.8 us -> 38.2 us  [local(): pl.pallas_call(kernel, out_shape=(jax.ShapeDtypeStruct((TOK, HEADS * VDIM...]
    unnamed x4 -> x2, local copies, waits for them, and re-layouts: 2.3 us -> 1.32 us
where the time goes in v3:
time: 40.2 us
  Pallas kernels  38.2 us (95%)
  local copies, waits for them, and re-layouts  1.32 us (3%)
  between operations  0.64 us (2%)
    pallas_call x1, Pallas kernels, local(): pl.pallas_call(kernel, out_shape=(jax.ShapeDtypeStruct((TOK, HEADS * VDIM...  38.2 us
    unnamed x2, local copies, waits for them, and re-layouts  1.32 us

profile of v3, /device:TPU:17, one launch (start us, length us, event | category | flops | bytes accessed | tf_op | source)
XLA Modules:
  0.0 40.2 jit_solution(16900496722637961061)
XLA Ops:
  0.6 38.2 %latent_attention.1 = (bf16[128,1024]{1,0:T(8,128)(2,1)S(1)}, bf16[32,640]{1,0:T(8,128)(2,1)S(1)}) custom-call(bf16[128,1024]{1,0:T(8,128)(2,1)} %qn_hbm.1, bf16[128,512]{1,0:T(8,128)(2,1)} %qr_hbm.1, bf16[16,576]{1,0:T(8,128)(2,1)} %kl_hbm.1, s32[16]{0:T(128)} %doc_hbm.1, s32[4]{0:T(128)} %off_hbm.1, s32[16]{0:T(128)} %bitcast.3, ...), custom_call_target="tpu_custom_call" | custom-call | tf_op jit(solution)/shard_map/latent_attention/pallas_call | solution.py:657
  38.8 0.7 %copy.12 = bf16[128,1024]{1,0:T(8,128)(2,1)} copy(bf16[128,1024]{1,0:T(8,128)(2,1)S(1)} %get-tuple-element.8) | data formatting | bytes 524288
  39.5 0.6 %copy.13 = bf16[32,576]{1,0:T(8,128)(2,1)} copy(bf16[32,576]{1,0:T(8,128)(2,1)S(1)} %bitcast.2) | data formatting | bytes 73728

commit v4 on v3

--- a/solution.py
+++ b/solution.py
@@ -555,11 +555,11 @@
     def _():
         help_first()
 
-    cache_middle()
     shared(1)
     sweep(1, wide_tiles)
-    for pos in range(6, 13):
+    for pos in (6, 10, 11, 12, 7, 8, 9):
         step(pos)
+    cache_middle()
     shared(2)
 
     @pl.when(helps)

time: 40.2 us -> 38.9 us (0.968)
  the two profiles are of different devices: /device:TPU:17 before, /device:TPU:41 now
where the time goes in v4:
time: 38.9 us; the launch traced here: 38.8 us
  Pallas kernels  36.9 us (95%)
  local copies, waits for them, and re-layouts  1.32 us (3%)
  between operations  0.64 us (2%)
    pallas_call x1, Pallas kernels, local(): pl.pallas_call(kernel, out_shape=(jax.ShapeDtypeStruct((TOK, HEADS * VDIM...  36.9 us
    unnamed x2, local copies, waits for them, and re-layouts  1.32 us

profile of v4, /device:TPU:41, one launch (start us, length us, event | category | flops | bytes accessed | tf_op | source)
XLA Modules:
  0.0 38.8 jit_solution(3251069207337316416)
XLA Ops:
  0.6 36.9 %latent_attention.1 = (bf16[128,1024]{1,0:T(8,128)(2,1)S(1)}, bf16[32,640]{1,0:T(8,128)(2,1)S(1)}) custom-call(bf16[128,1024]{1,0:T(8,128)(2,1)} %qn_hbm.1, bf16[128,512]{1,0:T(8,128)(2,1)} %qr_hbm.1, bf16[16,576]{1,0:T(8,128)(2,1)} %kl_hbm.1, s32[16]{0:T(128)} %doc_hbm.1, s32[4]{0:T(128)} %off_hbm.1, s32[16]{0:T(128)} %bitcast.3, ...), custom_call_target="tpu_custom_call" | custom-call | tf_op jit(solution)/shard_map/latent_attention/pallas_call | solution.py:657
  37.5 0.7 %copy.12 = bf16[128,1024]{1,0:T(8,128)(2,1)} copy(bf16[128,1024]{1,0:T(8,128)(2,1)S(1)} %get-tuple-element.8) | data formatting | bytes 524288
  38.2 0.6 %copy.13 = bf16[32,576]{1,0:T(8,128)(2,1)} copy(bf16[32,576]{1,0:T(8,128)(2,1)S(1)} %bitcast.2) | data formatting | bytes 73728
